TPU v7x, 256 devices: a whole 4x4x8 slice. The times are simulated.
256 devices in a mesh: row: 8 (over z), col: 32 (over y, x, core).
Axes of the slice: x: 4, y: 4, z: 8, core: 2. Of those that a mesh axis runs over, the one named last changes fastest.
Arguments:
- out_grads: bfloat16 [32, 48, 28672], P('col', None, 'row'), may hold values from -6 to 6
- acts: bfloat16 [32, 48, 8192], P('row', None, 'col'), may hold values from -6 to 6
- rot_out: bfloat16 [28672, 28672], P('row', 'col'), may hold values from -0.03125 to 0.03125
- rot_in: bfloat16 [8192, 8192], P('col', 'row'), may hold values from -0.0625 to 0.0625
- queries: bfloat16 [2, 28672, 8192], P(None, 'col', 'row'), may hold values from -0.00036621094 to 0.00036621094
- token_sequence: int32 [1024], replicated, may hold values from 0 to 31, never falling along the last dimension, each value on 1 to 48 neighbouring positions
Outputs:
- scores: float32 [1024, 2], P(('row', 'col'))
Inputs may be any that keep to these rules, and one draw needn't show every extreme that they name: `token_sequence`: values never fall along the tokens; every sequence 0 to 31 has 1 to 48 tokens, some sequence exactly 48; the k-th token of a sequence (from 0) sits in its slot k of out_grads and acts.
All inputs are finite; a program needn't handle non-finite values.
Results may differ from a plain program's by a relative error of at most 0.0041.
Values may be sent and summed in bfloat16 or wider, within the bound.
A program may use at most 128 MiB of HBM per device.

v0:
```python
import jax
import jax.numpy as jnp
from jax import lax
from jax.sharding import Mesh
from jax.sharding import PartitionSpec as P

COL = ("col_0", "col_1", "col_2")
ROW_COL = ("row", "col_0", "col_1", "col_2")


def copy_for_each(shard, axis):
    copies = jnp.broadcast_to(shard, (lax.axis_size(axis), *shard.shape))
    return lax.all_to_all(copies, axis, split_axis=0, concat_axis=0, tiled=True)


def laid_out(blocks, dim):
    lengths = list(blocks.shape[1:])
    lengths[dim] *= blocks.shape[0]
    return jnp.moveaxis(blocks, 0, dim).reshape(lengths)


def gathered_copies(shard, axis, dim):
    blocks = copy_for_each(shard, axis)
    return laid_out(blocks, dim)


def in_blocks(shard, dim, devices):
    lengths = shard.shape
    blocks = shard.reshape(*lengths[:dim], devices, lengths[dim] // devices, *lengths[dim + 1 :])
    return jnp.moveaxis(blocks, dim, 0)


def summed_on_arrival(shard, axis, dim):
    devices = lax.axis_size(axis)
    blocks = lax.all_to_all(in_blocks(shard, dim, devices), axis, 0, 0, tiled=True)
    return jnp.sum(blocks, axis=0)


def sum_by_chip_2(shard, chips, core, dim):
    sizes = (lax.axis_size(chips), lax.axis_size(core))
    blocks = in_blocks(shard, dim, sizes[0] * sizes[1])
    inside = blocks.shape[1:]
    blocks = blocks.reshape(*sizes, *inside).swapaxes(0, 1).reshape(-1, *inside)
    blocks = lax.psum_scatter(blocks, core, scatter_dimension=0, tiled=True)
    return lax.psum_scatter(blocks, chips, scatter_dimension=0, tiled=True)[0]


def token_places(token_sequence, seq_count, slot_count):
    token_count = token_sequence.shape[0]
    labels = jnp.arange(seq_count, dtype=jnp.int32)
    before = (token_sequence[:, None] < labels[None, :]).astype(jnp.int32)
    starts = jnp.sum(before, axis=0)
    member = (token_sequence[:, None] == labels[None, :]).astype(jnp.int32)
    own_start = jnp.sum(member * starts[None, :], axis=1)
    position = jnp.arange(token_count, dtype=jnp.int32) - own_start
    return token_sequence * slot_count + position


def local(out_grads, acts, rot_out, rot_in, queries, token_sequence):
    slot_count = out_grads.shape[1]
    seq_count = out_grads.shape[0] * lax.axis_size(COL)
    flat_index = token_places(token_sequence, seq_count, slot_count)
    act_slots = gathered_copies(acts, "row", 0)
    act_rows = jnp.take(
        act_slots.reshape(seq_count * slot_count, act_slots.shape[2]), flat_index, axis=0
    )
    piece = lax.all_gather(out_grads, COL, axis=0, tiled=True)
    flattened = piece.reshape(piece.shape[0] * piece.shape[1], piece.shape[2])
    slot_terms = jnp.dot(flattened, rot_out, preferred_element_type=jnp.float32)
    grad_terms = jnp.take(slot_terms, flat_index, axis=0)
    grad_share = summed_on_arrival(grad_terms, "row", 0).astype(jnp.bfloat16)
    rot_grads = gathered_copies(grad_share, "row", 0)
    act_share = sum_by_chip_2(
        jnp.dot(act_rows, rot_in, preferred_element_type=jnp.float32),
        ("col_0", "col_1"),
        "col_2",
        0,
    ).astype(jnp.bfloat16)
    rot_acts = gathered_copies(act_share, COL, 0)
    projected = jnp.einsum("tj,qij->tqi", rot_acts, queries, preferred_element_type=jnp.float32)
    score_terms = jnp.sum(projected * rot_grads[:, None, :], axis=2)
    return lax.psum_scatter(score_terms, ROW_COL, scatter_dimension=0, tiled=True)


def solution(mesh):
    torus = Mesh(
        mesh.devices.reshape(mesh.shape["row"], 4, 4, 2), ("row", "col_0", "col_1", "col_2")
    )
    in_specs = (
        P(COL, None, "row"),
        P("row", None, COL),
        P("row", COL),
        P(COL, "row"),
        P(None, COL, "row"),
        P(),
    )
    out_specs = P(ROW_COL, None)
    return jax.shard_map(local, mesh=torus, in_specs=in_specs, out_specs=out_specs, check_vma=False)
```

profile of v0, /device:TPU:1, one launch (start us, length us, event | category | flops | bytes accessed | tf_op | source)
XLA Modules:
  0.0 380.5 jit_solution(10519326108349929063)
XLA Ops:
  7.4 0.0 copy-start
  7.4 0.0 all-gather.2.cloned.1.call-start
  7.4 0.7 all-gather.2.cloned.1.call-update
  8.1 1.9 broadcast_in_dim.39
  9.9 9.0 %all-to-all-start = ((bf16[8,4,48,256]{3,2,1,0:T(8,128)(2,1)}), bf16[8,4,48,256]{3,2,1,0:T(8,128)(2,1)S(1)}, u32[]{:S(2)}, u32[]{:S(2)}) async-start(bf16[8,4,48,256]{3,2,1,0:T(8,128)(2,1)} %broadcast_in_dim.39), calls=%async_computation | async-start | bytes 1572864 | tf_op jit(solution)/shard_map/all_to_all | solution.py:13
  19.0 0.0 reduce-scatter.6.cloned.1.call-start
  19.0 0.8 convert_reduce_fusion
  19.8 0.8 select_reduce_fusion
  20.6 0.7 compare_and_fusion
  21.3 0.7 broadcast_clamp_fusion
  22.0 20.5 %all-to-all-done = bf16[8,4,48,256]{3,2,1,0:T(8,128)(2,1)S(1)} async-done(((bf16[8,4,48,256]{3,2,1,0:T(8,128)(2,1)}), bf16[8,4,48,256]{3,2,1,0:T(8,128)(2,1)S(1)}, u32[]{:S(2)}, u32[]{:S(2)}) %all-to-all-start) | async-done | bytes 786464 | tf_op jit(solution)/shard_map/all_to_all | solution.py:13
  42.5 3.9 %gather_fusion = bf16[1024,256]{1,0:T(8,128)(2,1)S(1)} fusion(bf16[1536,256]{1,0:T(8,128)(2,1)S(1)} %bitcast.24, s32[1024]{0:T(1024)S(1)} %broadcast_clamp_fusion), kind=kCustom, calls=%fused_computation | custom fusion | bytes 1052672 | tf_op jit(solution)/shard_map/jit(_take)/gather | solution.py:64
  46.5 0.0 copy-done
  46.5 0.8 fusion
  47.2 2.3 copy.14
  49.5 0.0 reduce-scatter.6.cloned.1.call-update
  49.5 29.5 %all-gather.2.cloned.1.call-done = bf16[32,48,3584]{2,1,0:T(8,128)(2,1)} async-done(((bf16[1,48,3584]{2,1,0:T(8,128)(2,1)}), bf16[32,48,3584]{2,1,0:T(8,128)(2,1)}) %all-gather.2.cloned.1.call-update) | async-done | bytes 11010064 | tf_op jit(solution)/shard_map/all_gather | solution.py:67
  79.1 17.0 %fusion.5 = f32[1536,896]{1,0:T(8,128)} fusion(bf16[1536,3584]{1,0:T(8,128)(2,1)} %bitcast.29, bf16[3584,896]{1,0:T(8,128)(2,1)} %param.8), kind=kOutput, calls=%fused_computation.19 | convolution fusion | flops 9865003008 | bytes 22937600 | tf_op jit(solution)/shard_map/dot_general | solution.py:69
  96.1 8.6 %gather_fusion.1 = f32[1024,896]{1,0:T(8,128)} fusion(f32[1536,896]{1,0:T(8,128)} %fusion.5, s32[1024]{0:T(1024)S(1)} %broadcast_clamp_fusion), kind=kCustom, calls=%fused_computation.1 | custom fusion | bytes 7344128 | tf_op jit(solution)/shard_map/jit(_take)/gather | solution.py:70
  104.7 4.2 %broadcast_select_fusion = f32[8,128,896]{2,1,0:T(8,128)} fusion(f32[8,128,896]{2,1,0:T(8,128)} %bitcast.27, pred[8,128]{1,0:T(8,128)(4,1)S(1)} %bitcast.28), kind=kLoop, calls=%fused_computation.4 | loop fusion | flops 917504 | bytes 7341056 | tf_op jit(solution)/shard_map/jit(_take)/select_n | solution.py:70
  108.9 6.7 %all-to-all-start.2 = ((f32[8,128,896]{2,1,0:T(8,128)}), f32[8,128,896]{2,1,0:T(8,128)}, u32[]{:S(2)}, u32[]{:S(2)}) async-start(f32[8,128,896]{2,1,0:T(8,128)} %broadcast_select_fusion), calls=%async_computation.3 | async-start | bytes 7340032 | tf_op jit(solution)/shard_map/all_to_all | solution.py:35
  115.6 0.0 reduce-scatter.8.cloned.1.call-start
  115.7 0.0 reduce-scatter.6.cloned.1.call-done
  115.7 0.5 reduce-scatter.8.cloned.1.call-update
  116.2 85.0 %all-to-all-done.2 = f32[8,128,896]{2,1,0:T(8,128)} async-done(((f32[8,128,896]{2,1,0:T(8,128)}), f32[8,128,896]{2,1,0:T(8,128)}, u32[]{:S(2)}, u32[]{:S(2)}) %all-to-all-start.2) | async-done | bytes 3670048 | tf_op jit(solution)/shard_map/all_to_all | solution.py:35
  201.2 2.2 reduce_sum.38
  203.5 0.2 copy.15
  203.7 1.5 broadcast_in_dim.46
  205.1 3.6 all-to-all-start.3
  208.7 0.0 reduce-scatter.8.cloned.1.call-done
  208.8 0.9 convert_bitcast_fusion
  209.7 42.1 %all-to-all-done.3 = bf16[8,128,896]{1,2,0:T(8,128)(2,1)S(1)} async-done(((bf16[8,128,896]{1,2,0:T(8,128)(2,1)}), bf16[8,128,896]{1,2,0:T(8,128)(2,1)S(1)}, u32[]{:S(2)}, u32[]{:S(2)}) %all-to-all-start.3) | async-done | bytes 1835040 | tf_op jit(solution)/shard_map/all_to_all | solution.py:13
  251.8 1.6 broadcast_in_dim.42
  253.4 8.6 %all-to-all-start.1 = ((bf16[32,32,1024]{2,1,0:T(8,128)(2,1)}), bf16[32,32,1024]{2,1,0:T(8,128)(2,1)}, u32[]{:S(2)}, u32[]{:S(2)}) async-start(bf16[32,32,1024]{2,1,0:T(8,128)(2,1)} %broadcast_in_dim.42), calls=%async_computation.2 | async-start | bytes 4194304 | tf_op jit(solution)/shard_map/all_to_all | solution.py:13
  262.0 2.7 copy.16
  264.7 3.6 bitcast_convert_fusion
  268.3 5.0 %copy.17 = f32[1024,896]{0,1:T(8,128)} copy(f32[1024,896]{1,0:T(8,128)} %bitcast_convert_fusion) | data formatting | bytes 7340032 | tf_op jit(solution)/shard_map/convert_element_type | solution.py:81
  273.3 16.6 %all-to-all-done.1 = bf16[32,32,1024]{2,1,0:T(8,128)(2,1)} async-done(((bf16[32,32,1024]{2,1,0:T(8,128)(2,1)}), bf16[32,32,1024]{2,1,0:T(8,128)(2,1)}, u32[]{:S(2)}, u32[]{:S(2)}) %all-to-all-start.1) | async-done | bytes 2097184 | tf_op jit(solution)/shard_map/all_to_all | solution.py:13
  289.9 0.0 copy-start.1
  289.9 7.8 %multiply_reduce_fusion = f32[1024,2]{0,1:T(2,128)S(1)} fusion(f32[1024,896]{0,1:T(8,128)} %copy.17, bf16[1024,1024,1]{1,0,2:T(8,128)(2,1)} %bitcast.6, bf16[2,896,1024]{2,1,0:T(8,128)(2,1)} %param.10), kind=kOutput, calls=%fused_computation.2 | convolution fusion | flops 3761764352 | bytes 9445376 | tf_op jit(solution)/shard_map/tj,qij->tqi/dot_general | solution.py:80
  297.8 74.6 %all-reduce.1 = f32[1024,2]{0,1:T(2,128)S(1)} all-reduce(f32[1024,2]{0,1:T(2,128)S(1)} %multiply_reduce_fusion), channel_id=4, replica_groups=mesh['row'=8,'col_0'=4,'col_1'=4,'col_2'=2] {'row','col_0','col_1','col_2'}, use_global_device_ids=true, to_apply=%region_6.7.clone | all-reduce | flops 2048 | bytes 16384
  372.4 0.6 constant_dynamic-slice_fusion
  373.0 0.0 copy-done.1
Async XLA Ops:
  7.4 39.1 %copy-start = (bf16[256,1024]{1,0:T(8,128)(2,1)S(1)}, bf16[256,1024]{1,0:T(8,128)(2,1)}, u32[]{:S(2)}) copy-start(bf16[256,1024]{1,0:T(8,128)(2,1)} %param.9) | copy-start | bytes 1572868
  7.4 71.7 %all-gather.2.cloned.1.call-start = ((), (), s32[]{:S(2)}) async-start(), calls=%async_computation.7 | async-start | bytes 11354112 | tf_op jit(solution)/shard_map/all_gather | solution.py:67
  9.9 32.6 %all-to-all-start = ((bf16[8,4,48,256]{3,2,1,0:T(8,128)(2,1)}), bf16[8,4,48,256]{3,2,1,0:T(8,128)(2,1)S(1)}, u32[]{:S(2)}, u32[]{:S(2)}) async-start(bf16[8,4,48,256]{3,2,1,0:T(8,128)(2,1)} %broadcast_in_dim.39), calls=%async_computation | async-start | bytes 1572864 | tf_op jit(solution)/shard_map/all_to_all | solution.py:13
  19.0 96.7 %reduce-scatter.6.cloned.1.call-start = ((), (), s32[]{:S(2)}) async-start(), calls=%async_computation.6 | async-start | bytes 6291456 | tf_op jit(solution)/shard_map/reduce_scatter | solution.py:44
  108.9 92.4 %all-to-all-start.2 = ((f32[8,128,896]{2,1,0:T(8,128)}), f32[8,128,896]{2,1,0:T(8,128)}, u32[]{:S(2)}, u32[]{:S(2)}) async-start(f32[8,128,896]{2,1,0:T(8,128)} %broadcast_select_fusion), calls=%async_computation.3 | async-start | bytes 7340032 | tf_op jit(solution)/shard_map/all_to_all | solution.py:35
  115.6 93.1 %reduce-scatter.8.cloned.1.call-start = ((), (), s32[]{:S(2)}) async-start(), calls=%async_computation.8 | async-start | bytes 2228224
  205.1 46.7 %all-to-all-start.3 = ((bf16[8,128,896]{1,2,0:T(8,128)(2,1)}), bf16[8,128,896]{1,2,0:T(8,128)(2,1)S(1)}, u32[]{:S(2)}, u32[]{:S(2)}) async-start(bf16[8,128,896]{1,2,0:T(8,128)(2,1)} %broadcast_in_dim.46), calls=%async_computation.4 | async-start | bytes 3670016 | tf_op jit(solution)/shard_map/all_to_all | solution.py:13
  253.4 36.5 %all-to-all-start.1 = ((bf16[32,32,1024]{2,1,0:T(8,128)(2,1)}), bf16[32,32,1024]{2,1,0:T(8,128)(2,1)}, u32[]{:S(2)}, u32[]{:S(2)}) async-start(bf16[32,32,1024]{2,1,0:T(8,128)(2,1)} %broadcast_in_dim.42), calls=%async_computation.2 | async-start | bytes 4194304 | tf_op jit(solution)/shard_map/all_to_all | solution.py:13
  289.9 83.1 %copy-start.1 = (bf16[256,1024]{1,0:T(8,128)(2,1)S(1)}, bf16[256,1024]{1,0:T(8,128)(2,1)}, u32[]{:S(2)}) copy-start(bf16[256,1024]{1,0:T(8,128)(2,1)} %param.9) | copy-start | bytes 1572868
Sparse Core Ops, SparseCore 0:
  10.7 68.2 all-gather.1
Sparse Core Ops, SparseCore 1:
  49.6 14.1 reduce-scatter.5
  120.1 77.6 reduce-scatter.7
where the time goes:
time: 381 us; the launch traced here: 380 us
  waiting for transfers between devices  195 us (51%)
  blocking collectives  74.6 us (20%)
  local copies, waits for them, and re-layouts  28.3 us (7%)
  starting transfers between devices  28 us (7%)
  matrix products  25.6 us (7%)
  between operations  14.9 us (4%)
  other arithmetic  13.8 us (4%)
    all_to_all x1, waiting for transfers between devices, summed_on_arrival(): lax.all_to_all(in_blocks(shard, dim, devices), axis, 0, 0, tiled=True)  85 us
    all_to_all x3, waiting for transfers between devices, copy_for_each(): return lax.all_to_all(copies, axis, split_axis=0, concat_axis=0, tiled=True)  79.3 us
    unnamed x1, blocking collectives  74.6 us
    all_gather x1, waiting for transfers between devices, local(): piece = lax.all_gather(out_grads, COL, axis=0, tiled=True)  29.5 us
    all_to_all x3, starting transfers between devices, copy_for_each(): return lax.all_to_all(copies, axis, split_axis=0, concat_axis=0, tiled=True)  21.2 us
    dot_general x1, matrix products, local(): slot_terms = jnp.dot(flattened, rot_out, preferred_element_type=jnp.float32)  17 us
    gather x1, local copies, waits for them, and re-layouts, local(): grad_terms = jnp.take(slot_terms, flat_index, axis=0)  8.63 us
    dot_general x1, matrix products, local(): jnp.einsum('tj,qij->tqi', rot_acts, queries, preferred_element_type=jnp.f...  7.84 us
  transfers between devices with their start and end apart: 7, of which 5 were waited for; matrix products, arithmetic and copies ran while one was open for 15% of the time, Pallas kernels for 0%

commit v1 on v0

--- a/solution.py
+++ b/solution.py
@@ -64,7 +64,9 @@
     act_rows = jnp.take(
         act_slots.reshape(seq_count * slot_count, act_slots.shape[2]), flat_index, axis=0
     )
-    piece = lax.all_gather(out_grads, COL, axis=0, tiled=True)
+    piece = jnp.concatenate(
+        lax.all_to_all(jnp.stack([out_grads] * lax.axis_size(COL)), COL, 0, 0), axis=0
+    )
     flattened = piece.reshape(piece.shape[0] * piece.shape[1], piece.shape[2])
     slot_terms = jnp.dot(flattened, rot_out, preferred_element_type=jnp.float32)
     grad_terms = jnp.take(slot_terms, flat_index, axis=0)

time: 381 us -> 486 us (1.28)
  waiting for transfers between devices: 195 us -> 260 us
  blocking collectives: 74.6 us -> 105 us
  starting transfers between devices: 28 us -> 36.4 us
  local copies, waits for them, and re-layouts: 28.3 us -> 33.8 us
    all_to_all x0 -> x1, waiting for transfers between devices: none -> 125 us  [local(): lax.all_to_all(jnp.stack([out_grads] * lax.axis_size(COL)), COL, 0, 0)]
    all_to_all x0 -> x1, blocking collectives: none -> 30.4 us  [copy_for_each(): return lax.all_to_all(copies, axis, split_axis=0, concat_axis=0, tiled=True)]
    all_gather x1 -> x0, waiting for transfers between devices: 29.5 us -> none  [local(): piece = lax.all_gather(out_grads, COL, axis=0, tiled=True)]
    all_to_all x3 -> x2, waiting for transfers between devices: 79.3 us -> 58.5 us  [copy_for_each(): return lax.all_to_all(copies, axis, split_axis=0, concat_axis=0, tiled=True)]
    all_to_all x0 -> x1, starting transfers between devices: none -> 9.72 us  [local(): lax.all_to_all(jnp.stack([out_grads] * lax.axis_size(COL)), COL, 0, 0)]
    all_to_all x1, waiting for transfers between devices: 85 us -> 75.9 us  [summed_on_arrival(): lax.all_to_all(in_blocks(shard, dim, devices), axis, 0, 0, tiled=True)]
    another operation x0 -> x1, local copies, waits for them, and re-layouts: none -> 6.25 us  [local(): jnp.stack([out_grads] * lax.axis_size(COL))]
    all_to_all x3 -> x2, starting transfers between devices: 21.2 us -> 22.1 us  [copy_for_each(): return lax.all_to_all(copies, axis, split_axis=0, concat_axis=0, tiled=True)]
  transfers between devices with their start and end apart: 7 -> 6, of which waited for: 5 -> 4; matrix products, arithmetic and copies ran while one was open for 15% -> 11% of each run, Pallas kernels for 0% -> 0%
where the time goes in v1:
time: 486 us
  waiting for transfers between devices  260 us (53%)
  blocking collectives  105 us (22%)
  starting transfers between devices  36.4 us (7%)
  local copies, waits for them, and re-layouts  33.8 us (7%)
  matrix products  25.6 us (5%)
  between operations  13.5 us (3%)
  other arithmetic  11.1 us (2%)
    all_to_all x1, waiting for transfers between devices, local(): lax.all_to_all(jnp.stack([out_grads] * lax.axis_size(COL)), COL, 0, 0)  125 us
    all_to_all x1, waiting for transfers between devices, summed_on_arrival(): lax.all_to_all(in_blocks(shard, dim, devices), axis, 0, 0, tiled=True)  75.9 us
    unnamed x1, blocking collectives  74.5 us
    all_to_all x2, waiting for transfers between devices, copy_for_each(): return lax.all_to_all(copies, axis, split_axis=0, concat_axis=0, tiled=True)  58.5 us
    all_to_all x1, blocking collectives, copy_for_each(): return lax.all_to_all(copies, axis, split_axis=0, concat_axis=0, tiled=True)  30.4 us
    all_to_all x2, starting transfers between devices, copy_for_each(): return lax.all_to_all(copies, axis, split_axis=0, concat_axis=0, tiled=True)  22.1 us
    dot_general x1, matrix products, local(): slot_terms = jnp.dot(flattened, rot_out, preferred_element_type=jnp.float32)  17 us
  transfers between devices with their start and end apart: 6, of which 4 were waited for; matrix products, arithmetic and copies ran while one was open for 11% of the time, Pallas kernels for 0%

profile of v1, /device:TPU:1, one launch (start us, length us, event | category | flops | bytes accessed | tf_op | source)
XLA Modules:
  0.0 485.6 jit_solution(9007129825620013311)
XLA Ops:
  6.5 0.0 copy-start
  6.5 1.0 broadcast_in_dim.39
  7.6 30.4 %all_to_all.25 = bf16[8,4,48,256]{3,2,1,0:T(8,128)(2,1)S(1)} all-to-all(bf16[8,4,48,256]{3,2,1,0:T(8,128)(2,1)S(1)} %broadcast_in_dim.39), channel_id=1, replica_groups=mesh['row'=8,'col_0'=4,'col_1'=4,'col_2'=2] {'row'}, dimensions={0} | all-to-all | bytes 1572864 | tf_op jit(solution)/shard_map/all_to_all | solution.py:13
  38.0 6.3 %stack.2 = bf16[32,1,48,3584]{3,2,1,0:T(8,128)(2,1)} broadcast(bf16[48,3584]{1,0:T(8,128)(2,1)} %bitcast.29), dimensions={2,3} | broadcast | bytes 11354112 | tf_op jit(solution)/shard_map/stack | solution.py:68
  44.2 0.0 copy-start.2
  44.2 9.7 %all-to-all-start.2 = ((bf16[32,1,48,3584]{3,2,1,0:T(8,128)(2,1)}), bf16[32,1,48,3584]{3,2,1,0:T(8,128)(2,1)}, u32[]{:S(2)}, u32[]{:S(2)}) async-start(bf16[32,1,48,3584]{3,2,1,0:T(8,128)(2,1)} %stack.2), calls=%async_computation.3 | async-start | bytes 22020096 | tf_op jit(solution)/shard_map/all_to_all | solution.py:68
  54.0 0.0 reduce-scatter.6.cloned.1.call-start
  54.0 0.0 copy-done.2
  54.0 0.1 convert_reduce_fusion
  54.1 0.1 select_reduce_fusion
  54.3 3.9 gather_fusion
  58.2 0.0 copy-done
  58.2 0.8 fusion
  59.0 2.3 copy.14
  61.3 0.0 reduce-scatter.6.cloned.1.call-update
  61.3 125.1 %all-to-all-done.2 = bf16[32,1,48,3584]{3,2,1,0:T(8,128)(2,1)} async-done(((bf16[32,1,48,3584]{3,2,1,0:T(8,128)(2,1)}), bf16[32,1,48,3584]{3,2,1,0:T(8,128)(2,1)}, u32[]{:S(2)}, u32[]{:S(2)}) %all-to-all-start.2) | async-done | bytes 11010080 | tf_op jit(solution)/shard_map/all_to_all | solution.py:68
  186.4 17.0 %fusion.5 = f32[1536,896]{1,0:T(8,128)} fusion(bf16[1536,3584]{1,0:T(8,128)(2,1)} %bitcast.9, bf16[3584,896]{1,0:T(8,128)(2,1)} %param.8), kind=kOutput, calls=%fused_computation.19 | convolution fusion | flops 9865003008 | bytes 22937600 | tf_op jit(solution)/shard_map/dot_general | solution.py:71
  203.5 8.6 %gather_fusion.1 = f32[1024,896]{1,0:T(8,128)} fusion(f32[1536,896]{1,0:T(8,128)} %fusion.5, s32[1024]{0:T(1024)S(1)} %broadcast_clamp_fusion), kind=kCustom, calls=%fused_computation.1 | custom fusion | bytes 7344128 | tf_op jit(solution)/shard_map/jit(_take)/gather | solution.py:72
  212.1 4.2 broadcast_select_fusion
  216.3 4.5 all-to-all-start.3
  220.8 0.0 reduce-scatter.8.cloned.1.call-start
  220.8 0.0 reduce-scatter.6.cloned.1.call-done
  220.9 0.7 reduce-scatter.8.cloned.1.call-update
  221.5 75.9 %all-to-all-done.3 = f32[8,128,896]{2,1,0:T(8,128)} async-done(((f32[8,128,896]{2,1,0:T(8,128)}), f32[8,128,896]{2,1,0:T(8,128)}, u32[]{:S(2)}, u32[]{:S(2)}) %all-to-all-start.3) | async-done | bytes 3670048 | tf_op jit(solution)/shard_map/all_to_all | solution.py:35
  297.5 2.2 reduce_sum.38
  299.7 0.2 copy.15
  299.9 1.5 broadcast_in_dim.46
  301.4 9.0 %all-to-all-start.4 = ((bf16[8,128,896]{1,2,0:T(8,128)(2,1)}), bf16[8,128,896]{1,2,0:T(8,128)(2,1)S(1)}, u32[]{:S(2)}, u32[]{:S(2)}) async-start(bf16[8,128,896]{1,2,0:T(8,128)(2,1)} %broadcast_in_dim.46), calls=%async_computation.5 | async-start | bytes 3670016 | tf_op jit(solution)/shard_map/all_to_all | solution.py:13
  310.4 0.0 reduce-scatter.8.cloned.1.call-done
  310.4 0.9 convert_bitcast_fusion
  311.3 42.0 %all-to-all-done.4 = bf16[8,128,896]{1,2,0:T(8,128)(2,1)S(1)} async-done(((bf16[8,128,896]{1,2,0:T(8,128)(2,1)}), bf16[8,128,896]{1,2,0:T(8,128)(2,1)S(1)}, u32[]{:S(2)}, u32[]{:S(2)}) %all-to-all-start.4) | async-done | bytes 1835040 | tf_op jit(solution)/shard_map/all_to_all | solution.py:13
  353.3 1.6 broadcast_in_dim.42
  354.9 13.1 %all-to-all-start.1 = ((bf16[32,32,1024]{2,1,0:T(8,128)(2,1)}), bf16[32,32,1024]{2,1,0:T(8,128)(2,1)}, u32[]{:S(2)}, u32[]{:S(2)}) async-start(bf16[32,32,1024]{2,1,0:T(8,128)(2,1)} %broadcast_in_dim.42), calls=%async_computation.2 | async-start | bytes 4194304 | tf_op jit(solution)/shard_map/all_to_all | solution.py:13
  368.0 2.7 copy.16
  370.7 3.6 bitcast_convert_fusion
  374.3 5.0 %copy.17 = f32[1024,896]{0,1:T(8,128)} copy(f32[1024,896]{1,0:T(8,128)} %bitcast_convert_fusion) | data formatting | bytes 7340032 | tf_op jit(solution)/shard_map/convert_element_type | solution.py:83
  379.3 16.5 %all-to-all-done.1 = bf16[32,32,1024]{2,1,0:T(8,128)(2,1)} async-done(((bf16[32,32,1024]{2,1,0:T(8,128)(2,1)}), bf16[32,32,1024]{2,1,0:T(8,128)(2,1)}, u32[]{:S(2)}, u32[]{:S(2)}) %all-to-all-start.1) | async-done | bytes 2097184 | tf_op jit(solution)/shard_map/all_to_all | solution.py:13
  395.8 0.0 copy-start.1
  395.8 7.8 %multiply_reduce_fusion = f32[1024,2]{0,1:T(2,128)S(1)} fusion(f32[1024,896]{0,1:T(8,128)} %copy.17, bf16[1024,1024,1]{1,0,2:T(8,128)(2,1)} %bitcast.6, bf16[2,896,1024]{2,1,0:T(8,128)(2,1)} %param.10), kind=kOutput, calls=%fused_computation.2 | convolution fusion | flops 3761764352 | bytes 9445376 | tf_op jit(solution)/shard_map/tj,qij->tqi/dot_general | solution.py:82
  403.7 74.5 %all-reduce.1 = f32[1024,2]{0,1:T(2,128)S(1)} all-reduce(f32[1024,2]{0,1:T(2,128)S(1)} %multiply_reduce_fusion), channel_id=4, replica_groups=mesh['row'=8,'col_0'=4,'col_1'=4,'col_2'=2] {'row','col_0','col_1','col_2'}, use_global_device_ids=true, to_apply=%region_6.7.clone | all-reduce | flops 2048 | bytes 16384
  478.2 0.6 constant_dynamic-slice_fusion
  478.8 0.0 copy-done.1
  (2 shorter events, 0.0 us)
Async XLA Ops:
  6.5 51.7 %copy-start = (bf16[256,1024]{1,0:T(8,128)(2,1)S(1)}, bf16[256,1024]{1,0:T(8,128)(2,1)}, u32[]{:S(2)}) copy-start(bf16[256,1024]{1,0:T(8,128)(2,1)} %param.9) | copy-start | bytes 1572868
  44.2 9.8 %copy-start.2 = (s32[1024]{0:T(1024)S(1)}, s32[1024]{0:T(1024)}, u32[]{:S(2)}) copy-start(s32[1024]{0:T(1024)} %param.11) | copy-start | bytes 12292
  44.2 142.2 %all-to-all-start.2 = ((bf16[32,1,48,3584]{3,2,1,0:T(8,128)(2,1)}), bf16[32,1,48,3584]{3,2,1,0:T(8,128)(2,1)}, u32[]{:S(2)}, u32[]{:S(2)}) async-start(bf16[32,1,48,3584]{3,2,1,0:T(8,128)(2,1)} %stack.2), calls=%async_computation.3 | async-start | bytes 22020096 | tf_op jit(solution)/shard_map/all_to_all | solution.py:68
  54.0 166.9 %reduce-scatter.6.cloned.1.call-start = ((), (), s32[]{:S(2)}) async-start(), calls=%async_computation.7 | async-start | bytes 6291456 | tf_op jit(solution)/shard_map/reduce_scatter | solution.py:44
  216.3 81.2 %all-to-all-start.3 = ((f32[8,128,896]{2,1,0:T(8,128)}), f32[8,128,896]{2,1,0:T(8,128)}, u32[]{:S(2)}, u32[]{:S(2)}) async-start(f32[8,128,896]{2,1,0:T(8,128)} %broadcast_select_fusion), calls=%async_computation.4 | async-start | bytes 7340032 | tf_op jit(solution)/shard_map/all_to_all | solution.py:35
  220.8 89.6 %reduce-scatter.8.cloned.1.call-start = ((), (), s32[]{:S(2)}) async-start(), calls=%async_computation.8 | async-start | bytes 2228224
  301.4 52.0 %all-to-all-start.4 = ((bf16[8,128,896]{1,2,0:T(8,128)(2,1)}), bf16[8,128,896]{1,2,0:T(8,128)(2,1)S(1)}, u32[]{:S(2)}, u32[]{:S(2)}) async-start(bf16[8,128,896]{1,2,0:T(8,128)(2,1)} %broadcast_in_dim.46), calls=%async_computation.5 | async-start | bytes 3670016 | tf_op jit(solution)/shard_map/all_to_all | solution.py:13
  354.9 40.9 %all-to-all-start.1 = ((bf16[32,32,1024]{2,1,0:T(8,128)(2,1)}), bf16[32,32,1024]{2,1,0:T(8,128)(2,1)}, u32[]{:S(2)}, u32[]{:S(2)}) async-start(bf16[32,32,1024]{2,1,0:T(8,128)(2,1)} %broadcast_in_dim.42), calls=%async_computation.2 | async-start | bytes 4194304 | tf_op jit(solution)/shard_map/all_to_all | solution.py:13
  395.8 83.0 %copy-start.1 = (bf16[256,1024]{1,0:T(8,128)(2,1)S(1)}, bf16[256,1024]{1,0:T(8,128)(2,1)}, u32[]{:S(2)}) copy-start(bf16[256,1024]{1,0:T(8,128)(2,1)} %param.9) | copy-start | bytes 1572868
Sparse Core Ops, SparseCore 0:
  61.5 13.9 reduce-scatter.5
  225.6 82.0 reduce-scatter.7
